TPU v7x, 32 devices: a whole 2x2x4 slice. The times are simulated.
32 devices in a mesh: dp: 4 (over z), vocab: 8 (over y, x, core).
Axes of the slice: x: 2, y: 2, z: 4, core: 2. Of those that a mesh axis runs over, the one named last changes fastest.
Arguments:
- tokens_in: bfloat16 [512, 8192], P('dp'), may hold values from -80 to 80
- gain: float32 [8192], replicated, may hold values from 0.5 to 1.5
- head_weight: bfloat16 [8192, 16896], P(None, 'vocab'), may hold values from -0.5 to 0.5
- teacher_ids: int32 [512, 16], P('dp'), may hold values from 0 to 16895
- teacher_weight: float32 [512, 16], P('dp'), may hold values from 0.05 to 1
- labels: int32 [512], P('dp'), may hold values from 0 to 16895
Outputs:
- token_loss: float32 [512], P('dp')
- grad_input: bfloat16 [512, 8192], P('dp', 'vocab')
- head_grad: float32 [2112, 8, 8192], P('dp', 'vocab')
All inputs are finite; a program needn't handle non-finite values.
Results may differ from a plain program's by a relative error of at most 0.015.
Values may be sent and summed in bfloat16 or wider, within the bound.
A program may use at most 192 MiB of HBM per device.

v0:
```python
import jax
import jax.numpy as jnp
from jax import lax
from jax.sharding import PartitionSpec as P

LABEL_SHARE = 0.5
EPS = 1e-05


def normalize(tokens_in, gain):
    as_float = tokens_in.astype(jnp.float32)
    row_scale = jnp.sqrt(jnp.mean(as_float * as_float, axis=1, keepdims=True) + EPS)
    normed = (as_float / row_scale * gain[None, :]).astype(jnp.bfloat16)
    return (as_float, row_scale, normed)


def targets(teacher_ids, teacher_probs, labels, col_start, col_width):
    columns = col_start + jnp.arange(col_width, dtype=jnp.int32)
    matches = (teacher_ids[:, :, None] == columns[None, None, :]).astype(jnp.float32)
    teacher_part = jnp.sum(teacher_probs[:, :, None] * matches, axis=1)
    label_part = (labels[:, None] == columns[None, :]).astype(jnp.float32)
    return (1.0 - LABEL_SHARE) * teacher_part + LABEL_SHARE * label_part


def head_part(dlogits, normed):
    head_term = lax.dot_general(
        dlogits, normed, (((0,), (0,)), ((), ())), preferred_element_type=jnp.float32
    )
    summed = lax.psum_scatter(
        head_term.astype(jnp.bfloat16), "dp", scatter_dimension=0, tiled=True
    ).astype(jnp.float32)
    return summed[:, None, :]


def input_part(dlogits, head_weight, as_float, row_scale, gain):
    partial_value = lax.dot_general(
        dlogits, head_weight, (((1,), (1,)), ((), ())), preferred_element_type=jnp.float32
    )
    dhidden = lax.psum_scatter(
        partial_value.astype(jnp.bfloat16), "vocab", scatter_dimension=1, tiled=True
    ).astype(jnp.float32)
    feature_count = as_float.shape[1]
    slice_width = dhidden.shape[1]
    slice_start = lax.axis_index("vocab") * slice_width
    local_tokens = lax.dynamic_slice_in_dim(as_float, slice_start, slice_width, 1)
    local_gain = lax.dynamic_slice_in_dim(gain, slice_start, slice_width, 0)
    scaled = dhidden * local_gain[None, :]
    inner_sum = lax.psum(jnp.sum(scaled * local_tokens, axis=1), "vocab")[:, None]
    cubed = row_scale * row_scale * row_scale
    return (scaled / row_scale - local_tokens * inner_sum / (feature_count * cubed)).astype(
        jnp.bfloat16
    )


def local(tokens_in, gain, head_weight, teacher_ids, teacher_weight, labels):
    col_width = head_weight.shape[1]
    col_start = lax.axis_index("vocab") * col_width
    as_float, row_scale, normed = normalize(tokens_in, gain)
    logits = jnp.dot(normed, head_weight, preferred_element_type=jnp.float32)
    teacher_probs = teacher_weight / jnp.sum(teacher_weight, axis=1, keepdims=True)
    target = targets(teacher_ids, teacher_probs, labels, col_start, col_width)
    local_dot = jnp.sum(target * logits, axis=1)
    row_top = lax.pmax(jnp.max(logits, axis=1), "vocab")
    total_exp, total_dot = lax.psum(
        (jnp.sum(jnp.exp(logits - row_top[:, None]), axis=1), local_dot), "vocab"
    )
    lse = row_top + jnp.log(total_exp)
    token_loss = (
        (1.0 - LABEL_SHARE) * jnp.sum(teacher_probs * jnp.log(teacher_probs), axis=1)
        - total_dot
        + lse
    )
    dlogits = (jnp.exp(logits - lse[:, None]) - target).astype(jnp.bfloat16)
    grad_input = input_part(dlogits, head_weight, as_float, row_scale, gain)
    head_grad = head_part(dlogits, normed)
    return (token_loss, grad_input, head_grad)


def solution(mesh):
    in_specs = (P("dp", None), P(), P(None, "vocab"), P("dp", None), P("dp", None), P("dp"))
    out_specs = (P("dp"), P("dp", "vocab"), P("dp", "vocab", None))
    return jax.shard_map(local, mesh=mesh, in_specs=in_specs, out_specs=out_specs, check_vma=False)
```

profile of v0, /device:TPU:0, one launch (start us, length us, event | category | flops | bytes accessed | tf_op | source)
XLA Modules:
  0.0 726.2 jit_solution(5216266142207354010)
XLA Ops:
  7.2 0.0 reduce-scatter.3.cloned.1.call-start
  7.2 2.2 multiply_reduce_fusion
  9.6 16.4 %fusion.3 = (f32[128]{0:T(128)S(1)}, f32[128,2112]{0,1:T(8,128)}) fusion(bf16[8192,2112]{0,1:T(8,128)(2,1)} %param.8, f32[8192]{0:T(1024)S(1)} %copy-done.3, f32[128]{0:T(128)S(1)} %get-tuple-element.16, bf16[128,8192]{1,0:T(8,128)(2,1)S(1)} %copy-done), kind=kOutput, calls=%fused_computation.23 | convolution fusion | flops 4433649664 | bytes 37815296 | tf_op jit(solution)/shard_map/dot_general | solution.py:59
  26.0 15.1 %pmax.7 = f32[128]{0:T(128)S(1)} all-reduce(f32[128]{0:T(128)S(1)} %get-tuple-element.17), channel_id=1, replica_groups=mesh['dp'=4,'vocab'=8] {'vocab'}, use_global_device_ids=true, to_apply=%region_7.0 | all-reduce | flops 128 | bytes 1024 | tf_op jit(solution)/shard_map/pmax | solution.py:63
  41.1 1.7 select_reduce_fusion
  42.8 2.1 multiply_reduce_fusion.1
  44.9 11.8 %psum.22 = f32[128]{0:T(128)S(1)} all-reduce(f32[128]{0:T(128)S(1)} %get-tuple-element.10), channel_id=1, replica_groups=mesh['dp'=4,'vocab'=8] {'vocab'}, use_global_device_ids=true, to_apply=%region_9.0 | all-reduce | flops 128 | bytes 1024 | tf_op jit(solution)/shard_map/psum | solution.py:64
  56.7 2.0 subtract_convert_fusion
  58.8 0.8 copy-done.1
  59.6 15.6 %convolution_convert_fusion.1 = bf16[128,8192]{1,0:T(8,128)(2,1)} fusion(bf16[128,2112]{0,1:T(8,128)(2,1)S(1)} %subtract_convert_fusion, bf16[8192,2112]{0,1:T(8,128)(2,1)} %param.8), kind=kOutput, calls=%fused_computation.2 | convolution fusion | flops 4430233600 | bytes 37240832 | tf_op jit(solution)/shard_map/dot_general | solution.py:36
  75.2 0.0 reduce-scatter.3.cloned.1.call-update
  75.2 0.2 reduce-scatter.5.cloned.1.call-start
  75.4 0.8 copy-done.2
  76.2 15.1 %convolution_convert_fusion = bf16[2112,8192]{1,0:T(8,128)(2,1)} fusion(bf16[128,2112]{0,1:T(8,128)(2,1)S(1)} %copy-done.2, f32[8192]{0:T(1024)S(1)} %copy-done.3, f32[128]{0:T(128)S(1)} %get-tuple-element.16, bf16[128,8192]{1,0:T(8,128)(2,1)S(1)} %copy-done), kind=kOutput, calls=%fused_computation | convolution fusion | flops 4450680832 | bytes 37274112 | tf_op jit(solution)/shard_map/dot_general | solution.py:26
  91.3 0.0 reduce-scatter.5.cloned.1.call-update
  91.3 2.4 convert_element_type.24
  93.8 22.2 %reduce-scatter.3.cloned.1.call-done = bf16[128,1024]{1,0:T(8,128)(2,1)} async-done(((bf16[128,8192]{1,0:T(8,128)(2,1)}), bf16[128,1024]{1,0:T(8,128)(2,1)}) %reduce-scatter.3.cloned.1.call-update) | async-done | bytes 262160 | tf_op jit(solution)/shard_map/reduce_scatter | solution.py:39
  116.0 1.3 multiply_reduce_fusion.2
  117.2 12.7 %all-reduce = (f32[128]{0:T(128)S(1)}, f32[128]{0:T(128)S(1)}) all-reduce(f32[128]{0:T(128)S(1)} %get-tuple-element.9, f32[128]{0:T(128)S(1)} %multiply_reduce_fusion.2), channel_id=1, replica_groups=mesh['dp'=4,'vocab'=8] {'vocab'}, use_global_device_ids=true, to_apply=%region_5.0 | all-reduce | flops 256 | bytes 2048 | tf_op jit(solution)/shard_map/psum | solution.py:64
  129.9 0.5 subtract_add_fusion
  130.4 2.0 subtract_convert_fusion.1
  132.4 554.9 %reduce-scatter.5.cloned.1.call-done = bf16[528,8192]{1,0:T(8,128)(2,1)} async-done(((bf16[2112,8192]{1,0:T(8,128)(2,1)}), bf16[528,8192]{1,0:T(8,128)(2,1)}) %reduce-scatter.5.cloned.1.call-update) | async-done | bytes 8650768 | tf_op jit(solution)/shard_map/reduce_scatter | solution.py:29
  687.3 11.6 %bitcast_convert_fusion = f32[528,1,8192]{2,0,1:T(8,128)} fusion(bf16[528,8192]{1,0:T(8,128)(2,1)} %reduce-scatter.5.cloned.1.call-done), kind=kLoop, calls=%fused_computation.3 | loop fusion | flops 4325376 | bytes 25952256 | tf_op jit(solution)/shard_map/broadcast_in_dim | solution.py:32
  699.0 20.4 %copy.12 = f32[528,1,8192]{2,1,0:T(1,128)} copy(f32[528,1,8192]{2,0,1:T(8,128)} %bitcast_convert_fusion) | data formatting | bytes 34603008
  (18 shorter events, 0.1 us)
Async XLA Ops:
  7.2 2.4 copy-start
  7.2 2.3 copy-start.4
  7.2 2.4 copy-start.3
  7.2 108.8 %reduce-scatter.3.cloned.1.call-start = ((), (), s32[]{:S(2)}) async-start(), calls=%async_computation.2 | async-start | bytes 2359296 | tf_op jit(solution)/shard_map/reduce_scatter | solution.py:39
  9.6 31.6 %copy-start.5 = (s32[128,16]{0,1:T(8,128)S(1)}, s32[128,16]{0,1:T(8,128)}, u32[]{:S(2)}) copy-start(s32[128,16]{0,1:T(8,128)} %param.9) | copy-start | bytes 24580
  9.6 33.3 %copy-start.6 = (s32[128]{0:T(128)S(1)}, s32[128]{0:T(128)}, u32[]{:S(2)}) copy-start(s32[128]{0:T(128)} %param.11) | copy-start | bytes 1540
  58.8 0.8 copy-start.1
  75.2 1.0 copy-start.2
  75.2 612.1 %reduce-scatter.5.cloned.1.call-start = ((), (), s32[]{:S(2)}) async-start(), calls=%async_computation.3 | async-start | bytes 43253760 | tf_op jit(solution)/shard_map/reduce_scatter | solution.py:29
Sparse Core Ops, SparseCore 0:
  75.3 40.5 reduce-scatter.2
  118.5 568.8 reduce-scatter.4
where the time goes:
time: 727 us; the launch traced here: 726 us
  waiting for transfers between devices  577 us (79%)
  matrix products  47.1 us (6%)
  blocking collectives  39.6 us (5%)
  other arithmetic  26 us (4%)
  local copies, waits for them, and re-layouts  22 us (3%)
  between operations  14.2 us (2%)
    reduce_scatter x1, waiting for transfers between devices, head_part(): lax.psum_scatter(head_term.astype(jnp.bfloat16), 'dp', scatter_dimension=...  555 us
    psum x2, blocking collectives, local(): lax.psum((jnp.sum(jnp.exp(logits - row_top[:, None]), axis=1), local_dot)...  24.5 us
    reduce_scatter x1, waiting for transfers between devices, input_part(): lax.psum_scatter(partial_value.astype(jnp.bfloat16), 'vocab', scatter_dim...  22.2 us
    unnamed x15, local copies, waits for them, and re-layouts  22 us
    dot_general x1, matrix products, local(): logits = jnp.dot(normed, head_weight, preferred_element_type=jnp.float32)  16.4 us
    dot_general x1, matrix products, input_part(): lax.dot_general(dlogits, head_weight, (((1,), (1,)), ((), ())), preferred...  15.6 us
    pmax x1, blocking collectives, local(): row_top = lax.pmax(jnp.max(logits, axis=1), 'vocab')  15.1 us
    dot_general x1, matrix products, head_part(): lax.dot_general(dlogits, normed, (((0,), (0,)), ((), ())), preferred_elem...  15.1 us
  transfers between devices with their start and end apart: 2, of which 2 were waited for; matrix products, arithmetic and copies ran while one was open for 3% of the time, Pallas kernels for 0%

commit v1 on v0

v1 whole, which is shorter than its diff:
```python
import jax
import jax.numpy as jnp
from jax import lax
from jax.sharding import PartitionSpec as P

LABEL_SHARE = 0.5
EPS = 1e-05


def normalize(tokens_in, gain):
    as_float = tokens_in.astype(jnp.float32)
    row_scale = jnp.sqrt(jnp.mean(as_float * as_float, axis=1, keepdims=True) + EPS)
    normed = (as_float / row_scale * gain[None, :]).astype(jnp.bfloat16)
    return (as_float, row_scale, normed)


def targets(teacher_ids, teacher_probs, labels, col_start, col_width):
    columns = col_start + jnp.arange(col_width, dtype=jnp.int32)
    matches = (teacher_ids[:, :, None] == columns[None, None, :]).astype(jnp.float32)
    teacher_part = jnp.sum(teacher_probs[:, :, None] * matches, axis=1)
    label_part = (labels[:, None] == columns[None, :]).astype(jnp.float32)
    return (1.0 - LABEL_SHARE) * teacher_part + LABEL_SHARE * label_part


def local(tokens_in, gain, head_weight, teacher_ids, teacher_weight, labels):
    features, col_width = head_weight.shape
    slice_width = features // lax.axis_size("vocab")
    here = lax.axis_index("vocab")
    col_start = here * col_width
    slice_start = here * slice_width
    local_tokens = lax.dynamic_slice_in_dim(tokens_in, slice_start, slice_width, 1)
    mine = lax.all_gather(local_tokens, "dp", axis=0, tiled=True)
    everyone = lax.all_gather(mine, "vocab", axis=1, tiled=True)

    as_float, row_scale, normed = normalize(tokens_in, gain)
    logits = jnp.dot(normed, head_weight, preferred_element_type=jnp.float32)
    teacher_probs = teacher_weight / jnp.sum(teacher_weight, axis=1, keepdims=True)
    target = targets(teacher_ids, teacher_probs, labels, col_start, col_width)
    local_dot = jnp.sum(target * logits, axis=1)
    local_top = jnp.max(logits, axis=1)
    expo = jnp.exp(logits - local_top[:, None])
    stats = jnp.stack([local_top, jnp.sum(expo, axis=1), local_dot, jnp.sum(expo * logits, axis=1)])
    stats = lax.all_gather(stats, "vocab", axis=0)
    row_top = jnp.max(stats[:, 0], axis=0)
    shrink = jnp.exp(stats[:, 0] - row_top[None, :])
    total_exp = jnp.sum(stats[:, 1] * shrink, axis=0)
    total_dot = jnp.sum(stats[:, 2], axis=0)
    mean_logit = jnp.sum(stats[:, 3] * shrink, axis=0) / total_exp
    lse = row_top + jnp.log(total_exp)
    token_loss = (
        (1.0 - LABEL_SHARE) * jnp.sum(teacher_probs * jnp.log(teacher_probs), axis=1)
        - total_dot
        + lse
    )
    dlogits = (jnp.exp(logits - lse[:, None]) - target).astype(jnp.bfloat16)
    all_dlogits = lax.all_to_all(dlogits, "dp", split_axis=1, concat_axis=0, tiled=True)

    partial_value = lax.dot_general(
        dlogits, head_weight, (((1,), (1,)), ((), ())), preferred_element_type=jnp.float32
    )
    dhidden = lax.psum_scatter(
        partial_value.astype(jnp.bfloat16), "vocab", scatter_dimension=1, tiled=True
    ).astype(jnp.float32)
    local_gain = lax.dynamic_slice_in_dim(gain, slice_start, slice_width, 0)
    scaled = dhidden * local_gain[None, :]
    inner_over_scale = (mean_logit - total_dot)[:, None]
    grad_input = (
        scaled / row_scale
        - local_tokens.astype(jnp.float32) * inner_over_scale / (features * row_scale * row_scale)
    ).astype(jnp.bfloat16)

    _, _, all_normed = normalize(everyone, gain)
    head_grad = lax.dot_general(
        all_dlogits, all_normed, (((0,), (0,)), ((), ())), preferred_element_type=jnp.float32
    )
    return (token_loss, grad_input, head_grad[:, None, :])


def solution(mesh):
    in_specs = (P("dp", None), P(), P(None, "vocab"), P("dp", None), P("dp", None), P("dp"))
    out_specs = (P("dp"), P("dp", "vocab"), P("dp", "vocab", None))
    return jax.shard_map(local, mesh=mesh, in_specs=in_specs, out_specs=out_specs, check_vma=False)
```

time: 727 us -> 223 us (0.31)
  waiting for transfers between devices: 577 us -> 122 us
  blocking collectives: 39.6 us -> 10.4 us
  other arithmetic: 26 us -> 14.3 us
  matrix products: 47.1 us -> 38 us
    reduce_scatter x2 -> x1, waiting for transfers between devices: 577 us -> 41.6 us  [local(): lax.psum_scatter(partial_value.astype(jnp.bfloat16), 'vocab', scatter_dim...]
    all_gather x0 -> x2, waiting for transfers between devices: none -> 80.4 us  [the longest x1 52.3 us: local(): everyone = lax.all_gather(mine, 'vocab', axis=1, tiled=True)]
    psum x2 -> x0, blocking collectives: 24.5 us -> none  [local(): lax.psum((jnp.sum(jnp.exp(logits - row_top[:, None]), axis=1), local_dot)...]
    pmax x1 -> x0, blocking collectives: 15.1 us -> none  [local(): row_top = lax.pmax(jnp.max(logits, axis=1), 'vocab')]
    broadcast_in_dim x1 -> x0, other arithmetic: 11.6 us -> none  [head_part(): return summed[:, None, :]]
    all_gather x0 -> x1, blocking collectives: none -> 10.4 us  [local(): stats = lax.all_gather(stats, 'vocab', axis=0)]
    dot_general x2, matrix products: 30.7 us -> 22.4 us  [the longest x1 15 us: local(): lax.dot_general(dlogits, head_weight, (((1,), (1,)), ((), ())), preferred...]
    unnamed x15 -> x9, local copies, waits for them, and re-layouts: 22 us -> 20.8 us
  transfers between devices with their start and end apart: 2 -> 4, of which waited for: 2 -> 3; matrix products, arithmetic and copies ran while one was open for 3% -> 2% of each run, Pallas kernels for 0% -> 0%
where the time goes in v1:
time: 223 us
  waiting for transfers between devices  122 us (55%)
  matrix products  38 us (17%)
  local copies, waits for them, and re-layouts  20.8 us (9%)
  other arithmetic  14.3 us (6%)
  between operations  13.9 us (6%)
  blocking collectives  10.4 us (5%)
  starting transfers between devices  3.79 us (2%)
    all_gather x1, waiting for transfers between devices, local(): everyone = lax.all_gather(mine, 'vocab', axis=1, tiled=True)  52.3 us
    reduce_scatter x1, waiting for transfers between devices, local(): lax.psum_scatter(partial_value.astype(jnp.bfloat16), 'vocab', scatter_dim...  41.6 us
    all_gather x1, waiting for transfers between devices, local(): mine = lax.all_gather(local_tokens, 'dp', axis=0, tiled=True)  28.1 us
    unnamed x9, local copies, waits for them, and re-layouts  20.8 us
    dot_general x1, matrix products, local(): logits = jnp.dot(normed, head_weight, preferred_element_type=jnp.float32)  15.6 us
    dot_general x1, matrix products, local(): lax.dot_general(dlogits, head_weight, (((1,), (1,)), ((), ())), preferred...  15 us
    all_gather x1, blocking collectives, local(): stats = lax.all_gather(stats, 'vocab', axis=0)  10.4 us
    dot_general x1, matrix products, local(): lax.dot_general(all_dlogits, all_normed, (((0,), (0,)), ((), ())), prefer...  7.39 us
  transfers between devices with their start and end apart: 4, of which 3 were waited for; matrix products, arithmetic and copies ran while one was open for 2% of the time, Pallas kernels for 0%

profile of v1, /device:TPU:0, one launch (start us, length us, event | category | flops | bytes accessed | tf_op | source)
XLA Modules:
  0.0 223.2 jit_solution(12546026626790089893)
XLA Ops:
  7.2 0.0 reduce-scatter.2.cloned.1.call-start
  7.2 2.1 fusion.6
  9.4 1.7 select_reduce_fusion
  11.1 0.0 copy-start.2
  11.2 15.6 %fusion.18 = (f32[128]{0:T(128)S(1)}, f32[128,2112]{0,1:T(8,128)S(1)}) fusion(bf16[8192,2112]{0,1:T(8,128)(2,1)} %param.8, bf16[128,8192]{1,0:T(8,128)(2,1)} %param.6, f32[8192]{0:T(1024)S(1)} %copy-done.3, f32[128]{0:T(128)S(1)} %get-tuple-element.32), kind=kOutput, calls=%fused_computation.44 | convolution fusion | flops 4433649664 | bytes 37815296 | tf_op jit(solution)/shard_map/dot_general | solution.py:36
  26.8 1.0 fusion.13
  27.8 10.4 %all-gather.1 = f32[8,4,128]{2,1,0:T(4,128)S(1)} all-gather(f32[1,4,128]{2,1,0:T(4,128)S(1)} %maximum_bitcast_fusion), channel_id=2, replica_groups=mesh['dp'=4,'vocab'=8] {'vocab'}, dimensions={0}, use_global_device_ids=true | all-gather | bytes 18432 | tf_op jit(solution)/shard_map/all_gather | solution.py:43
  38.3 0.5 subtract_add_fusion
  38.8 1.7 subtract_convert_fusion
  40.5 15.0 %convolution_convert_fusion = bf16[128,8192]{1,0:T(8,128)(2,1)} fusion(bf16[128,2112]{0,1:T(8,128)(2,1)} %subtract_convert_fusion, bf16[8192,2112]{0,1:T(8,128)(2,1)} %param.8), kind=kOutput, calls=%fused_computation.7 | convolution fusion | flops 4430233600 | bytes 37240832 | tf_op jit(solution)/shard_map/dot_general | solution.py:58
  55.5 0.0 reduce-scatter.2.cloned.1.call-update
  55.5 0.0 all-gather.5.cloned.1.call-start
  55.6 41.6 %reduce-scatter.2.cloned.1.call-done = bf16[128,1024]{1,0:T(8,128)(2,1)} async-done(((bf16[128,8192]{1,0:T(8,128)(2,1)}), bf16[128,1024]{1,0:T(8,128)(2,1)}) %reduce-scatter.2.cloned.1.call-update) | async-done | bytes 262160 | tf_op jit(solution)/shard_map/reduce_scatter | solution.py:61
  97.2 2.0 subtract_convert_fusion.1
  99.2 0.0 all-gather.5.cloned.1.call-update
  99.2 0.0 all-gather.7.cloned.1.call-start
  99.3 28.1 %all-gather.5.cloned.1.call-done = bf16[512,1024]{1,0:T(8,128)(2,1)} async-done(((bf16[128,1024]{1,0:T(8,128)(2,1)}), bf16[512,1024]{1,0:T(8,128)(2,1)}) %all-gather.5.cloned.1.call-update) | async-done | bytes 1048592 | tf_op jit(solution)/shard_map/all_gather | solution.py:32
  127.4 0.0 all-gather.7.cloned.1.call-update
  127.4 3.7 %all-to-all-start = ((bf16[128,4,528]{0,2,1:T(8,128)(2,1)}), bf16[128,4,528]{0,2,1:T(8,128)(2,1)S(1)}, u32[]{:S(2)}, u32[]{:S(2)}) async-start(bf16[128,4,528]{0,2,1:T(8,128)(2,1)} %bitcast.8), calls=%async_computation.1 | async-start | bytes 1081344 | tf_op jit(solution)/shard_map/all_to_all | solution.py:56
  131.0 52.3 %all-gather.7.cloned.1.call-done = bf16[512,8192]{1,0:T(8,128)(2,1)} async-done(((bf16[512,1024]{1,0:T(8,128)(2,1)}), bf16[512,8192]{1,0:T(8,128)(2,1)}) %all-gather.7.cloned.1.call-update) | async-done | bytes 8388624 | tf_op jit(solution)/shard_map/all_gather | solution.py:33
  183.3 5.1 %fusion = f32[512]{0:T(512)S(1)} fusion(bf16[512,8192]{1,0:T(8,128)(2,1)} %all-gather.7.cloned.1.call-done), kind=kLoop, calls=%fused_computation.3 | loop fusion | flops 12582400 | bytes 8390656 | tf_op jit(solution)/shard_map/reduce_sum | solution.py:12
  188.5 0.0 all-to-all-done
  188.5 7.4 %convolution_bitcast_fusion = f32[528,1,8192]{2,0,1:T(8,128)S(1)} fusion(bf16[512,8192]{1,0:T(8,128)(2,1)} %all-gather.7.cloned.1.call-done, f32[8192]{0:T(1024)S(1)} %copy-done.3, f32[512]{0:T(512)S(1)} %add_sqrt_fusion, bf16[128,4,528]{0,2,1:T(8,128)(2,1)S(1)} %all-to-all-done), kind=kOutput, calls=%fused_computation.6 | convolution fusion | flops 4445962240 | bytes 26265600 | tf_op jit(solution)/shard_map/dot_general | solution.py:73
  195.9 20.8 %copy.29 = f32[528,1,8192]{2,1,0:T(1,128)} copy(f32[528,1,8192]{2,0,1:T(8,128)S(1)} %convolution_bitcast_fusion) | data formatting | bytes 34603008
  (17 shorter events, 0.2 us)
Async XLA Ops:
  7.2 2.2 copy-start
  7.2 2.2 %copy-start.1 = (s32[128,16]{0,1:T(8,128)S(1)}, s32[128,16]{0,1:T(8,128)}, u32[]{:S(2)}) copy-start(s32[128,16]{0,1:T(8,128)} %param.9) | copy-start | bytes 24580
  7.2 3.9 %copy-start.3 = (f32[8192]{0:T(1024)S(1)}, f32[8192]{0:T(1024)}, u32[]{:S(2)}) copy-start(f32[8192]{0:T(1024)} %param.7) | copy-start | bytes 98308
  7.2 90.0 %reduce-scatter.2.cloned.1.call-start = ((), (), s32[]{:S(2)}) async-start(), calls=%async_computation.2 | async-start | bytes 2359296 | tf_op jit(solution)/shard_map/reduce_scatter | solution.py:61
  11.1 15.7 %copy-start.2 = (s32[128]{0:T(128)S(1)}, s32[128]{0:T(128)}, u32[]{:S(2)}) copy-start(s32[128]{0:T(128)} %param.11) | copy-start | bytes 1540
  55.5 71.9 %all-gather.5.cloned.1.call-start = ((), (), s32[]{:S(2)}) async-start(), calls=%async_computation.3 | async-start | bytes 1310720 | tf_op jit(solution)/shard_map/all_gather | solution.py:32
  99.2 84.1 %all-gather.7.cloned.1.call-start = ((), (), s32[]{:S(2)}) async-start(), calls=%async_computation.4 | async-start | bytes 9437184 | tf_op jit(solution)/shard_map/all_gather | solution.py:33
  127.4 61.1 %all-to-all-start = ((bf16[128,4,528]{0,2,1:T(8,128)(2,1)}), bf16[128,4,528]{0,2,1:T(8,128)(2,1)S(1)}, u32[]{:S(2)}, u32[]{:S(2)}) async-start(bf16[128,4,528]{0,2,1:T(8,128)(2,1)} %bitcast.8), calls=%async_computation.1 | async-start | bytes 1081344 | tf_op jit(solution)/shard_map/all_to_all | solution.py:56
Sparse Core Ops, SparseCore 0:
  55.6 41.5 reduce-scatter.1
  99.4 27.9 all-gather.4
  129.4 53.8 all-gather.6

commit v2 on v1

--- a/solution.py
+++ b/solution.py
@@ -1,6 +1,10 @@
+import functools
+
 import jax
 import jax.numpy as jnp
 from jax import lax
+from jax.experimental import pallas as pl
+from jax.experimental.pallas import tpu as pltpu
 from jax.sharding import PartitionSpec as P
 
 LABEL_SHARE = 0.5
@@ -76,7 +80,340 @@
     return (token_loss, grad_input, head_grad[:, None, :])
 
 
+MESH = pl.DeviceIdType.MESH
+VMEM_BYTES = 60 * 1024 * 1024
+
+
+def fused_kernel(
+    nz, nv,
+    normed, xs, gs, rs, target, entropy, w_hbm,
+    loss_o, gin_o, gath_o, dlt_o,
+    w_v, logits_v, dl_v, dlt_v, scol, stat_s, stat_r, send_p, recv_p, own, send_c, recv_c,
+    w_sem, z_send, z_recv, f_send, f_recv, k_send, k_recv, st_send, st_recv,
+    d_send, d_recv, p_send, p_recv, c_send, c_recv, loc_sem,
+):
+    tok, features = normed.shape
+    cols = w_hbm.shape[1]
+    nc = nv // 2
+    slw = features // nv
+    half = features // 2
+    share = cols // nz
+    z = lax.axis_index("dp")
+    p = lax.axis_index("vocab")
+    chip, core = p // 2, p % 2
+    partner = chip * 2 + (1 - core)
+
+    def chip_at(step):
+        return lax.rem(chip + step, nc)
+
+    def z_at(step):
+        return lax.rem(z + step, nz)
+
+    barrier = pltpu.get_barrier_semaphore()
+    for r in range(1, nz):
+        pl.semaphore_signal(barrier, inc=1, device_id={"dp": z_at(r)}, device_id_type=MESH)
+    for r in range(1, nv):
+        pl.semaphore_signal(
+            barrier, inc=1, device_id={"vocab": lax.rem(p + r, nv)}, device_id_type=MESH
+        )
+
+    chunk = 512
+    n_chunks = features // chunk
+
+    def w_copy(k):
+        rows = pl.ds(pl.multiple_of(k * chunk, chunk), chunk)
+        return pltpu.make_async_copy(w_hbm.at[rows, :], w_v.at[rows, :], w_sem.at[k])
+
+    @pl.loop(0, n_chunks)
+    def _(k):
+        w_copy(k).start()
+
+    pl.semaphore_wait(barrier, nz - 1 + nv - 1)
+
+    def rows_of(zz):
+        return pl.ds(pl.multiple_of(zz * tok, tok), tok)
+
+    def slice_of(c, k):
+        return pl.ds(pl.multiple_of((k * nc + c) * slw, slw), slw)
+
+    def half_of(k):
+        return pl.ds(pl.multiple_of(k * half, half), half)
+
+    def z_copy(r):
+        return pltpu.make_async_remote_copy(
+            normed.at[:, slice_of(chip, core)],
+            gath_o.at[rows_of(z), slice_of(chip, core)],
+            z_send.at[r], z_recv.at[r], device_id={"dp": z_at(r)}, device_id_type=MESH,
+        )
+
+    def f_copy(r, step):
+        region = gath_o.at[rows_of(z_at(nz - r)), slice_of(chip, core)]
+        return pltpu.make_async_remote_copy(
+            region, region, f_send.at[r, step], f_recv.at[r, step],
+            device_id={"vocab": chip_at(step) * 2 + core}, device_id_type=MESH,
+        )
+
+    def k_copy(r):
+        region = gath_o.at[rows_of(z_at(nz - r)), half_of(core)]
+        return pltpu.make_async_remote_copy(
+            region, region, k_send.at[r], k_recv.at[r],
+            device_id={"vocab": partner}, device_id_type=MESH,
+        )
+
+    order = sorted(range(1, nz), key=lambda r: (min(r, nz - r), r))
+
+    def forward(r):
+        z_copy(r).wait_recv()
+        for step in range(1, nc):
+            f_copy(r, step).start()
+
+    def forward_core(r):
+        for step in range(1, nc):
+            f_copy(r, step).wait_recv()
+        k_copy(r).start()
+
+    for r in order:
+        z_copy(r).start()
+    mine = pltpu.make_async_copy(normed, gath_o.at[rows_of(z), :], loc_sem.at[0])
+    mine.start()
+
+    logits_v[...] = jnp.zeros_like(logits_v)
+
+    def logit_chunk(k):
+        w_copy(k).wait()
+        rows = pl.ds(pl.multiple_of(k * chunk, chunk), chunk)
+        logits_v[:, :cols] += jnp.dot(
+            normed[:, rows], w_v[rows, :], preferred_element_type=jnp.float32
+        )
+
+    pl.loop(0, n_chunks // 2)(logit_chunk)
+    forward(order[0])
+    pl.loop(n_chunks // 2, n_chunks)(logit_chunk)
+
+    group = 16
+
+    @pl.loop(0, tok // group)
+    def _(g):
+        rows = pl.ds(pl.multiple_of(g * group, group), group)
+        lg = logits_v[rows, :cols]
+        top = jnp.max(lg, axis=1, keepdims=True)
+        expo = jnp.exp(lg - top)
+        lane = lax.broadcasted_iota(jnp.int32, (group, 128), 1)
+        total = jnp.sum(expo, axis=1, keepdims=True)
+        dot = jnp.sum(target[rows, :] * lg, axis=1, keepdims=True)
+        weighted = jnp.sum(expo * lg, axis=1, keepdims=True)
+        scol[rows, :] = jnp.where(
+            lane == 0, top, jnp.where(lane == 1, total, jnp.where(lane == 2, dot, weighted))
+        )
+
+    stat_s[...] = jnp.transpose(scol[...])[:8]
+
+    def st_copy(r):
+        return pltpu.make_async_remote_copy(
+            stat_s, stat_r.at[r], st_send.at[r], st_recv.at[r],
+            device_id={"vocab": lax.rem(p + r, nv)}, device_id_type=MESH,
+        )
+
+    for r in range(1, nv):
+        st_copy(r).start()
+    for r in order[1:2]:
+        forward(r)
+    for r in range(1, nv):
+        st_copy(r).wait_recv()
+    stats = [stat_s[...]] + [stat_r[r] for r in range(1, nv)]
+    row_top = functools.reduce(jnp.maximum, [s[0:1] for s in stats])
+    shrink = [jnp.exp(s[0:1] - row_top) for s in stats]
+    total_exp = sum(s[1:2] * f for s, f in zip(stats, shrink))
+    total_dot = sum(s[2:3] for s in stats)
+    mean_logit = sum(s[3:4] * f for s, f in zip(stats, shrink)) / total_exp
+    lse = row_top + jnp.log(total_exp)
+    loss_o[...] = entropy[...] - total_dot + lse
+    sub = lax.broadcasted_iota(jnp.int32, (tok, tok), 0)
+    back = jnp.where(sub == 0, lse, mean_logit - total_dot)
+    scol[...] = jnp.transpose(back)
+
+    @pl.loop(0, tok // group)
+    def _(g):
+        rows = pl.ds(pl.multiple_of(g * group, group), group)
+        dl = jnp.exp(logits_v[rows, :cols] - scol[rows, 0:1]) - target[rows, :]
+        logits_v[rows, :cols] = dl
+        dl_v[rows, :] = dl.astype(jnp.bfloat16)
+
+    for c in range((cols + 127) // 128):
+        size = min(128, cols - c * 128)
+        block = jnp.transpose(logits_v[:, c * 128:(c + 1) * 128])
+        dlt_v[c * 128:c * 128 + size, :] = block[:size].astype(jnp.bfloat16)
+
+    def share_of(zz):
+        return pl.ds(pl.multiple_of(zz * share, 16), share)
+
+    def d_copy(r):
+        return pltpu.make_async_remote_copy(
+            dlt_v.at[share_of(z_at(r)), :], dlt_o.at[:, rows_of(z)],
+            d_send.at[r], d_recv.at[r], device_id={"dp": z_at(r)}, device_id_type=MESH,
+        )
+
+    for r in order:
+        d_copy(r).start()
+    mine_d = pltpu.make_async_copy(dlt_v.at[share_of(z), :], dlt_o.at[:, rows_of(z)], loc_sem.at[1])
+    mine_d.start()
+    for r in order[2:]:
+        forward(r)
+
+    def p_copy(step):
+        return pltpu.make_async_remote_copy(
+            send_p.at[step], recv_p.at[step], p_send.at[step], p_recv.at[step],
+            device_id={"vocab": partner}, device_id_type=MESH,
+        )
+
+    def c_copy(step):
+        return pltpu.make_async_remote_copy(
+            send_c.at[step], recv_c.at[step], c_send.at[step], c_recv.at[step],
+            device_id={"vocab": chip_at(step) * 2 + core}, device_id_type=MESH,
+        )
+
+    tile = 256
+
+    def product(step, which, dest):
+        start = (chip_at(step) * 2 + which) * slw
+
+        @pl.loop(0, slw // tile)
+        def _(j):
+            rows = pl.ds(pl.multiple_of(start + j * tile, tile), tile)
+            here = pl.ds(pl.multiple_of(j * tile, tile), tile)
+            dest[step, :, here] = lax.dot_general(
+                dl_v[...], w_v[rows, :], (((1,), (1,)), ((), ())),
+                preferred_element_type=jnp.float32,
+            ).astype(dest.dtype)
+
+    def pass_on(step):
+        p_copy(step).wait_recv()
+        send_c[step] = (own[step] + recv_p[step].astype(jnp.float32)).astype(jnp.bfloat16)
+        c_copy(step).start()
+
+    steps = list(range(1, nc)) + [0]
+    for at, step in enumerate(steps):
+        product(step, 1 - core, send_p)
+        p_copy(step).start()
+        product(step, core, own)
+        if at > 0:
+            pass_on(steps[at - 1])
+
+    for r in order:
+        forward_core(r)
+    p_copy(0).wait_recv()
+    for step in range(1, nc):
+        c_copy(step).wait_recv()
+
+    @pl.loop(0, tok // group)
+    def _(g):
+        rows = pl.ds(pl.multiple_of(g * group, group), group)
+        dh = own[0, rows, :] + recv_p[0, rows, :].astype(jnp.float32)
+        for step in range(1, nc):
+            dh += recv_c[step, rows, :].astype(jnp.float32)
+        scale = rs[rows, 0:1]
+        inner = scol[rows, 1:2] / (features * scale * scale)
+        gin_o[rows, :] = (
+            dh * gs[...] / scale - xs[rows, :].astype(jnp.float32) * inner
+        ).astype(jnp.bfloat16)
+
+    for r in order:
+        k_copy(r).wait()
+        d_copy(r).wait()
+        z_copy(r).wait_send()
+        for step in range(1, nc):
+            f_copy(r, step).wait_send()
+    for r in range(1, nv):
+        st_copy(r).wait_send()
+    for step in range(nc):
+        p_copy(step).wait_send()
+    for step in range(1, nc):
+        c_copy(step).wait_send()
+    mine.wait()
+    mine_d.wait()
+
+
+def head_kernel(a_ref, n_ref, out_ref):
+    out_ref[:, 0, :] = jnp.dot(a_ref[...], n_ref[...], preferred_element_type=jnp.float32)
+
+
+def local_fused(nz, nv, tokens_in, gain, head_weight, teacher_ids, teacher_weight, labels):
+    features, cols = head_weight.shape
+    tok = tokens_in.shape[0]
+    slw, share, nc = features // nv, cols // nz, nv // 2
+    here = lax.axis_index("vocab")
+    _, row_scale, normed = normalize(tokens_in, gain)
+    teacher_probs = teacher_weight / jnp.sum(teacher_weight, axis=1, keepdims=True)
+    target = targets(teacher_ids, teacher_probs, labels, here * cols, cols)
+    entropy = (1.0 - LABEL_SHARE) * jnp.sum(teacher_probs * jnp.log(teacher_probs), axis=1)
+    xs = lax.dynamic_slice_in_dim(tokens_in, here * slw, slw, 1)
+    gs = lax.dynamic_slice_in_dim(gain, here * slw, slw, 0)
+    vmem = pl.BlockSpec(memory_space=pltpu.VMEM)
+    hbm = pl.BlockSpec(memory_space=pl.ANY)
+    dma = pltpu.SemaphoreType.DMA
+    loss, grad_input, gathered, dlt = pl.pallas_call(
+        functools.partial(fused_kernel, nz, nv),
+        out_shape=(
+            jax.ShapeDtypeStruct((1, tok), jnp.float32),
+            jax.ShapeDtypeStruct((tok, slw), jnp.bfloat16),
+            jax.ShapeDtypeStruct((nz * tok, features), jnp.bfloat16),
+            jax.ShapeDtypeStruct((share, nz * tok), jnp.bfloat16),
+        ),
+        in_specs=[vmem] * 6 + [hbm],
+        out_specs=(vmem, vmem, hbm, hbm),
+        scratch_shapes=[
+            pltpu.VMEM((features, cols), jnp.bfloat16),
+            pltpu.VMEM((tok, (cols + 127) // 128 * 128), jnp.float32),
+            pltpu.VMEM((tok, cols), jnp.bfloat16),
+            pltpu.VMEM((cols, tok), jnp.bfloat16),
+            pltpu.VMEM((tok, 128), jnp.float32),
+            pltpu.VMEM((8, tok), jnp.float32),
+            pltpu.VMEM((nv, 8, tok), jnp.float32),
+            pltpu.VMEM((nc, tok, slw), jnp.bfloat16),
+            pltpu.VMEM((nc, tok, slw), jnp.bfloat16),
+            pltpu.VMEM((nc, tok, slw), jnp.float32),
+            pltpu.VMEM((nc, tok, slw), jnp.bfloat16),
+            pltpu.VMEM((nc, tok, slw), jnp.bfloat16),
+            dma((features // 512,)),
+            dma((nz,)), dma((nz,)), dma((nz, nc)), dma((nz, nc)), dma((nz,)), dma((nz,)),
+            dma((nv,)), dma((nv,)), dma((nz,)), dma((nz,)),
+            dma((nc,)), dma((nc,)), dma((nc,)), dma((nc,)), dma((2,)),
+        ],
+        compiler_params=pltpu.CompilerParams(
+            collective_id=0, has_side_effects=True, vmem_limit_bytes=VMEM_BYTES
+        ),
+        name="fused",
+    )(normed, xs, gs[None, :], row_scale, target, entropy[None, :], head_weight)
+
+    width = 1024
+    head_grad = pl.pallas_call(
+        head_kernel,
+        grid=(features // width,),
+        out_shape=jax.ShapeDtypeStruct((share, 1, features), jnp.float32),
+        in_specs=[
+            pl.BlockSpec((share, nz * tok), lambda j: (0, 0)),
+            pl.BlockSpec((nz * tok, width), lambda j: (0, j)),
+        ],
+        out_specs=pl.BlockSpec((share, 1, width), lambda j: (0, 0, j)),
+        compiler_params=pltpu.CompilerParams(vmem_limit_bytes=VMEM_BYTES),
+        name="head",
+    )(dlt, gathered)
+    return (loss[0], grad_input, head_grad)
+
+
 def solution(mesh):
+    nz, nv = mesh.shape["dp"], mesh.shape["vocab"]
+
+    def choose(tokens_in, gain, head_weight, *rest):
+        tok, (features, cols) = tokens_in.shape[0], head_weight.shape
+        aligned = (
+            tok == 128 and nv % 2 == 0 and features % (nv * 256) == 0 and cols % (nz * 16) == 0
+        )
+        fits = nz * tok * features <= 1 << 23 and features * cols <= 1 << 25
+        if aligned and fits:
+            return local_fused(nz, nv, tokens_in, gain, head_weight, *rest)
+        return local(tokens_in, gain, head_weight, *rest)
+
     in_specs = (P("dp", None), P(), P(None, "vocab"), P("dp", None), P("dp", None), P("dp"))
     out_specs = (P("dp"), P("dp", "vocab"), P("dp", "vocab", None))
-    return jax.shard_map(local, mesh=mesh, in_specs=in_specs, out_specs=out_specs, check_vma=False)
+    return jax.shard_map(choose, mesh=mesh, in_specs=in_specs, out_specs=out_specs, check_vma=False)

time: 223 us -> 140 us (0.63)
  waiting for transfers between devices: 122 us -> 0 us
  Pallas kernels: 0 us -> 79.8 us
  matrix products: 38 us -> 0 us
  local copies, waits for them, and re-layouts: 20.8 us -> 48.2 us
  between operations: 13.9 us -> 0.72 us
  blocking collectives: 10.4 us -> 0 us
  other arithmetic: 14.3 us -> 9.32 us
  starting transfers between devices: 3.79 us -> 0 us
    all_gather x2 -> x0, waiting for transfers between devices: 80.4 us -> none  [the longest x1 52.3 us: local(): everyone = lax.all_gather(mine, 'vocab', axis=1, tiled=True)]
    pallas_call x0 -> x2, Pallas kernels: none -> 79.8 us  [the longest x1 65.9 us: local_fused(): pl.pallas_call(functools.partial(fused_kernel, nz, nv), out_shape=(jax.Sh...]
    reduce_scatter x1 -> x0, waiting for transfers between devices: 41.6 us -> none  [local(): lax.psum_scatter(partial_value.astype(jnp.bfloat16), 'vocab', scatter_dim...]
    dot_general x3 -> x0, matrix products: 38 us -> none  [the longest x1 15.6 us: local(): logits = jnp.dot(normed, head_weight, preferred_element_type=jnp.float32)]
    unnamed x9 -> x17, local copies, waits for them, and re-layouts: 20.8 us -> 43.8 us
    all_gather x1 -> x0, blocking collectives: 10.4 us -> none  [local(): stats = lax.all_gather(stats, 'vocab', axis=0)]
    reduce_sum x2 -> x1, other arithmetic: 7.18 us -> 2.08 us  [normalize(): jnp.mean(as_float * as_float, axis=1, keepdims=True) + EPS]
    all_to_all x1 -> x0, starting transfers between devices: 3.66 us -> none  [local(): lax.all_to_all(dlogits, 'dp', split_axis=1, concat_axis=0, tiled=True)]
  transfers between devices with their start and end apart: 4 -> 0, of which waited for: 3 -> 0; matrix products, arithmetic and copies ran while one was open for 2% -> 0% of each run, Pallas kernels for 0% -> 0%
where the time goes in v2:
time: 140 us; the launch traced here: 138 us
  Pallas kernels  79.8 us (57%)
  local copies, waits for them, and re-layouts  48.2 us (34%)
  other arithmetic  9.32 us (7%)
    pallas_call x1, Pallas kernels, local_fused(): pl.pallas_call(functools.partial(fused_kernel, nz, nv), out_shape=(jax.Sh...  65.9 us
    unnamed x17, local copies, waits for them, and re-layouts  43.8 us
    pallas_call x1, Pallas kernels, local_fused(): pl.pallas_call(head_kernel, grid=(features // width,), out_shape=jax.Shap...  13.9 us

profile of v2, /device:TPU:0, one launch (start us, length us, event | category | flops | bytes accessed | tf_op | source)
XLA Modules:
  0.0 138.0 jit_solution(16878102401559497877)
XLA Ops:
  0.6 0.0 copy-start
  0.6 0.0 copy-start.3
  0.7 0.0 copy-start.4
  0.7 0.9 reduce_sum.37
  1.5 2.1 %fusion = f32[128]{0:T(128)S(1)} fusion(bf16[128,8192]{1,0:T(8,128)(2,1)} %param.6), kind=kLoop, calls=%fused_computation.3 | loop fusion | flops 3145600 | bytes 2097664 | tf_op jit(solution)/shard_map/reduce_sum | solution.py:16
  3.6 0.0 copy-start.5
  3.6 1.3 dynamic_slice.7
  4.9 0.0 copy-done.3
  4.9 0.5 multiply_bitcast_fusion.entropy
  5.5 0.7 copy.14.rs
  6.2 0.0 copy-done
  6.2 0.7 constant_dynamic-slice_fusion.xs
  6.9 0.0 copy-done.4
  6.9 2.7 %select_reduce_fusion = f32[128,2112]{0,1:T(8,128)} fusion(f32[128,16]{0,1:T(8,128)S(1)} %get-tuple-element.12, s32[128,16]{0,1:T(8,128)S(1)} %copy-done.4, s32[2112]{0:T(1024)S(1)} %iota_add_fusion), kind=kLoop, calls=%fused_computation | loop fusion | flops 12705792 | bytes 1106176 | tf_op jit(solution)/shard_map/reduce_sum | solution.py:24
  9.6 1.6 %copy.13 = f32[128,2112]{1,0:T(8,128)S(1)} copy(f32[128,2112]{0,1:T(8,128)} %select_reduce_fusion) | data formatting | bytes 2162688 | tf_op jit(solution)/shard_map/reduce_sum | solution.py:24
  11.2 0.0 copy-done.5
  11.2 1.2 select_add_fusion.target
  12.5 0.0 copy-done.2
  12.5 1.9 %fusion.2.normed = bf16[128,8192]{1,0:T(8,128)(2,1)} fusion(bf16[128,8192]{1,0:T(8,128)(2,1)S(1)} %copy-done, f32[8192]{0:T(1024)S(1)} %copy-done.2, f32[128]{0:T(128)S(1)} %get-tuple-element.14), kind=kLoop, calls=%fused_computation.5 | loop fusion | flops 4194304 | bytes 4227584 | tf_op jit(solution)/shard_map/convert_element_type | solution.py:17
  14.4 42.6 %copy.15.w_hbm = bf16[8192,2112]{1,0:T(8,128)(2,1)} copy(bf16[8192,2112]{0,1:T(8,128)(2,1)} %param.8) | data formatting | bytes 69206016 | tf_op args[2]
  57.0 65.9 %fused.1 = (f32[1,128]{1,0:T(1,128)}, bf16[128,1024]{1,0:T(8,128)(2,1)}, bf16[512,8192]{1,0:T(8,128)(2,1)}, bf16[528,512]{1,0:T(8,128)(2,1)}) custom-call(bf16[128,8192]{1,0:T(8,128)(2,1)} %fusion.2.normed, bf16[128,1024]{1,0:T(8,128)(2,1)} %constant_dynamic-slice_fusion.xs, f32[1,1024]{1,0:T(1,128)} %bitcast.6, f32[128,1]{1,0:T(8,128)} %copy.14.rs, ...), custom_call_target="tpu_custom_call" | custom-call | tf_op jit(solution)/shard_map/fused/pallas_call | solution.py:354
  122.9 13.9 %head.1 = f32[528,1,8192]{2,1,0:T(1,128)} custom-call(bf16[528,512]{1,0:T(8,128)(2,1)} %get-tuple-element.9.a_ref, bf16[512,8192]{1,0:T(8,128)(2,1)} %get-tuple-element.10.n_ref), custom_call_target="tpu_custom_call" | custom-call | tf_op jit(solution)/shard_map/head/pallas_call | solution.py:389
  136.8 0.5 copy.18
  137.3 0.7 copy.19
  (8 shorter events, 0.0 us)
Async XLA Ops:
  0.6 5.6 %copy-start = (bf16[128,8192]{1,0:T(8,128)(2,1)S(1)}, bf16[128,8192]{1,0:T(8,128)(2,1)}, u32[]{:S(2)}) copy-start(bf16[128,8192]{1,0:T(8,128)(2,1)} %param.6) | copy-start | bytes 6291460
  0.6 4.3 %copy-start.3 = (f32[128,16]{0,1:T(8,128)S(1)}, f32[128,16]{0,1:T(8,128)}, u32[]{:S(2)}) copy-start(f32[128,16]{0,1:T(8,128)} %param.10) | copy-start | bytes 24580
  0.7 6.3 %copy-start.4 = (s32[128,16]{0,1:T(8,128)S(1)}, s32[128,16]{0,1:T(8,128)}, u32[]{:S(2)}) copy-start(s32[128,16]{0,1:T(8,128)} %param.9) | copy-start | bytes 24580
  3.6 7.6 %copy-start.5 = (s32[128]{0:T(128)S(1)}, s32[128]{0:T(128)}, u32[]{:S(2)}) copy-start(s32[128]{0:T(128)} %param.11) | copy-start | bytes 1540
  9.6 2.8 %copy-start.2 = (f32[8192]{0:T(1024)S(1)}, f32[8192]{0:T(1024)}, u32[]{:S(2)}) copy-start(f32[8192]{0:T(1024)} %param.7) | copy-start | bytes 98308
  122.9 13.9 %copy-start.6 = (f32[1,128]{1,0:T(1,128)S(1)}, f32[1,128]{1,0:T(1,128)}, u32[]{:S(2)}) copy-start(f32[1,128]{1,0:T(1,128)} %get-tuple-element.7) | copy-start | bytes 1540
  122.9 14.4 %copy-start.1 = (bf16[128,1024]{1,0:T(8,128)(2,1)S(1)}, bf16[128,1024]{1,0:T(8,128)(2,1)}, u32[]{:S(2)}) copy-start(bf16[128,1024]{1,0:T(8,128)(2,1)} %get-tuple-element.19) | copy-start | bytes 786436
